TPU v7x, 32 devices: a whole 2x2x4 slice. The times are simulated.
32 devices in a mesh: dom: 4 (over z), hid: 4 (over x, core), wt: 2 (over y).
Axes of the slice: x: 2, y: 2, z: 4, core: 2. Of those that a mesh axis runs over, the one named last changes fastest.
Arguments:
- store_feat: bfloat16 [16384, 256], P('dom'), may hold values from -6 to 6
- want_in: int32 [4, 4, 128], P('dom'), may hold values from 0 to 4095
- nbr_in: int32 [32768, 10], P('dom'), may hold values from 0 to 511
- self_in: int32 [32768], P('dom'), may hold values from 0 to 511
- count_in: int32 [32768], P('dom'), may hold values from 1 to 10
- weight_one: bfloat16 [512, 1024], P('wt', 'hid'), may hold values from -0.375 to 0.375
- want_hid: int32 [4, 4, 128], P('dom'), may hold values from 0 to 8191
- nbr_hid: int32 [8192, 15], P('dom'), may hold values from 0 to 511
- self_hid: int32 [8192], P('dom'), may hold values from 0 to 511
- count_hid: int32 [8192], P('dom'), may hold values from 1 to 15
- weight_two: bfloat16 [2048, 1024], P('wt', 'hid'), may hold values from -0.1875 to 0.1875
Outputs:
- seed_embed: bfloat16 [8192, 1024], P('dom', 'hid')
Inputs may be any that keep to these rules, and one draw needn't show every extreme that they name: `count_in`: slots at or past a node's count hold arbitrary positions and are ignored. `count_hid`: slots at or past a seed's count hold arbitrary positions and are ignored.
All inputs are finite; a program needn't handle non-finite values.
Results may differ from a plain program's by a relative error of at most 0.0052.
Values may be sent and summed in bfloat16 or wider, within the bound.
A program may use at most 128 MiB of HBM per device.

v0:
```python
import functools
import math

import jax
import jax.numpy as jnp
from jax import lax
from jax.experimental import pallas as pl
from jax.experimental.pallas import tpu as pltpu
from jax.sharding import PartitionSpec as P

F32 = jnp.float32
BF16 = jnp.bfloat16
I32 = jnp.int32
BLOCK = 256


def product(a, b):
    return jnp.dot(a, b, preferred_element_type=F32)


def tally(spots, first, last, block, weight=None):
    shifted = (spots - (block * BLOCK).astype(F32)).astype(BF16)
    lanes = lax.broadcasted_iota(I32, (spots.shape[0], BLOCK), 1).astype(F32).astype(BF16)
    one, none = jnp.ones((), BF16), jnp.zeros((), BF16)
    total = jnp.zeros(lanes.shape, BF16)
    for column in range(first, last):
        hit = jnp.broadcast_to(shifted[:, column : column + 1], lanes.shape) == lanes
        total = total + jnp.where(hit, one if weight is None else weight, none)
    return total


def kernel(
    shape,
    want_in, want_hid, store, nbr_in, self_in, count_in, w_one, nbr_hid, self_hid, count_hid, w_two,
    out,
    storef, nodes, table, picked, fetched, w_first, w_second, hidden, first_c, full, rows, seeds, second_c,
    local_sem, w_send, w_recv, f_send, f_recv, fc_send, fc_recv, h_send, h_recv, g_send, g_recv,
):
    doms, fan_one, fan_two = shape
    me, h, w = lax.axis_index("dom"), lax.axis_index("hid"), lax.axis_index("wt")
    core = lax.rem(h, 2)
    mate = {"hid": h + 1 - 2 * core}
    side_h = lax.rem(h + 2, 4)
    side = {"hid": side_h}
    over = {"wt": 1 - w}

    def remote(src, dst, send, recv, where):
        return pltpu.make_async_remote_copy(
            src_ref=src, dst_ref=dst, send_sem=send, recv_sem=recv,
            device_id=where, device_id_type=pl.DeviceIdType.MESH,
        )

    barrier = pltpu.get_barrier_semaphore()
    for where in (mate, side, over):
        pl.semaphore_signal(barrier, inc=1, device_id=where, device_id_type=pl.DeviceIdType.MESH)

    @pl.loop(1, doms)
    def _(s):
        pl.semaphore_signal(
            barrier, inc=1, device_id={"dom": lax.rem(me + s, doms)}, device_id_type=pl.DeviceIdType.MESH
        )

    half, features = picked.shape[1], picked.shape[2]
    fetch = want_hid.shape[1]
    width = w_first.shape[2]

    @pl.loop(0, store.shape[0], step=256)
    def _(start):
        start = pl.multiple_of(start, 256)
        storef[pl.ds(start, 256), :] = store[pl.ds(start, 256), :].astype(F32)

    @pl.loop(0, doms)
    def _(p):
        @pl.loop(0, half, step=16)
        def _(start):
            start = pl.multiple_of(start, 16)
            got = [storef[pl.ds(want_in[p, core * half + start + i], 1), :] for i in range(16)]
            picked[p, pl.ds(start, 16), :] = jnp.concatenate(got, 0).astype(BF16)

    pl.semaphore_wait(barrier, doms + 2)

    def fetch_copy(s, q, p):
        return remote(picked.at[p], fetched.at[q, core], f_send.at[s], f_recv.at[s], {"dom": p})

    def pass_copy(q, c):
        return remote(fetched.at[q, c], fetched.at[q, c], fc_send.at[q], fc_recv.at[q], mate)

    @pl.loop(1, doms)
    def _(s):
        fetch_copy(s, me, lax.rem(me + s, doms)).start()

    fetched[me, core] = picked[me]
    pass_copy(me, core).start()

    their_columns = pl.ds(pl.multiple_of((1 - w) * width, width), width)
    my_columns = pl.ds(pl.multiple_of(w * width, width), width)
    one_copy = remote(w_one.at[:, their_columns], w_first.at[w], w_send.at[0], w_recv.at[0], over)
    two_copy = remote(w_two, w_second.at[w], w_send.at[1], w_recv.at[1], over)
    one_copy.start()
    two_copy.start()
    local_one = pltpu.make_async_copy(w_one.at[:, my_columns], w_first.at[w], local_sem.at[0])
    local_two = pltpu.make_async_copy(w_two, w_second.at[w], local_sem.at[1])
    local_one.start()
    local_two.start()

    def slots(neighbours, own, counts, fan, span):
        number = counts[:, span]
        order = lax.broadcasted_iota(I32, (fan, number.shape[1]), 0)
        valid = jnp.where(order < number, neighbours[:, span], -1)
        lines = [valid.astype(F32), own[:, span].astype(F32), number.astype(F32)]
        pad = -(fan + 2) % 8
        if pad:
            lines.append(jnp.zeros((pad, number.shape[1]), F32))
        return jnp.concatenate(lines, 0).T

    @pl.loop(0, nodes.shape[0], step=512)
    def _(start):
        span = pl.ds(pl.multiple_of(start, 512), 512)
        nodes[span, :] = slots(nbr_in, self_in, count_in, fan_one, span)

    @pl.loop(0, doms)
    def _(p):
        @pl.loop(0, fetch, step=8)
        def _(start):
            start = pl.multiple_of(start, 8)
            got = [nodes[pl.ds(want_hid[p, start + i], 1), :] for i in range(8)]
            table[pl.ds(pl.multiple_of(p * fetch, 8) + start, 8), :] = jnp.concatenate(got, 0)

    @pl.loop(0, seeds.shape[0], step=512)
    def _(start):
        span = pl.ds(pl.multiple_of(start, 512), 512)
        seeds[span, :] = slots(nbr_hid, self_hid, count_hid, fan_two, span)

    def lanes_of(block):
        return pl.ds(pl.multiple_of(block * BLOCK, BLOCK), BLOCK)

    looked = doms * fetched.shape[1] * half
    group = math.gcd(doms, 4)
    step_rows = group * fetch

    def count_nodes(start):
        @pl.loop(0, step_rows, step=64)
        def _(part):
            part = pl.multiple_of(part, 64)
            spots = table[pl.ds(start + part, 64), :]

            @pl.loop(0, looked // BLOCK)
            def _(block):
                first_c[pl.ds(part, 64), lanes_of(block)] = tally(spots, 0, fan_one, block)
                there = pl.ds(pl.multiple_of(looked + block * BLOCK, BLOCK), BLOCK)
                first_c[pl.ds(part, 64), there] = tally(spots, fan_one, fan_one + 1, block)

    known = rows.shape[0] // 2

    def count_seeds(first, last, base):
        @pl.loop(first, last, step=64)
        def _(part):
            part = pl.multiple_of(part, 64)
            spots = seeds[pl.ds(part, 64), :]
            number = spots[:, fan_two + 1 : fan_two + 2].astype(BF16)

            @pl.loop(0, known // BLOCK)
            def _(block):
                there = pl.ds(pl.multiple_of(known + block * BLOCK, BLOCK), BLOCK)
                second_c[pl.ds(part - base, 64), lanes_of(block)] = tally(
                    spots, fan_two, fan_two + 1, block, number
                )
                second_c[pl.ds(part - base, 64), there] = tally(spots, 0, fan_two, block)

    small = doms == group
    total_seeds = seeds.shape[0]
    early = total_seeds // 2
    if small:
        count_nodes(0)

    @pl.loop(1, doms)
    def _(s):
        q = lax.rem(me - s + doms, doms)
        fetch_copy(s, q, lax.rem(me + s, doms)).wait_recv()
        pass_copy(q, core).start()

    if small:
        count_seeds(0, early, 0)

    @pl.loop(0, doms)
    def _(q):
        pass_copy(q, 1 - core).wait_recv()

    local_one.wait()
    one_copy.wait_recv()

    @pl.loop(0, doms // group)
    def _(part):
        start = pl.multiple_of(part * step_rows, step_rows)
        if not small:
            count_nodes(start)
        lookup = fetched[...].reshape(looked, features)
        number = table[pl.ds(start, step_rows), fan_one + 1 : fan_one + 2]
        mean = (product(first_c[:, :looked], lookup) / number).astype(BF16)
        own = product(first_c[:, looked:], lookup).astype(BF16)
        made = product(own, w_first[0]) + product(mean, w_first[1])
        made = jnp.maximum(made, 0.0).astype(BF16)
        for i in range(group):
            hidden[part * group + i] = made[i * fetch : (i + 1) * fetch]

    def columns_of(hh, ww):
        return pl.ds(pl.multiple_of((hh * 2 + ww) * width, width), width)

    mine, beside, across = columns_of(h, w), columns_of(side_h, w), columns_of(h, 1 - w)
    corner = columns_of(side_h, 1 - w)
    mate_h = h + 1 - 2 * core
    mate_side = lax.rem(mate_h + 2, 4)
    theirs = [
        columns_of(mate_h, w), columns_of(mate_side, w), columns_of(mate_h, 1 - w), columns_of(mate_side, 1 - w)
    ]

    def hidden_copy(s, q, p):
        return remote(hidden.at[p], full.at[q, :, mine], h_send.at[s], h_recv.at[s], {"dom": p})

    def plane(q, k, view, where):
        return remote(full.at[q, view[0], view[1]], full.at[q, view[0], view[1]], g_send.at[q, k], g_recv.at[q, k], where)

    everything, upper, lower = pl.ds(0, fetch), pl.ds(0, fetch // 2), pl.ds(fetch // 2, fetch // 2)

    def spread(q):
        plane(q, 0, (everything, mine), side).start()
        plane(q, 1, (everything, mine), over).start()
        plane(q, 4, (everything, mine), mate).start()

    @pl.loop(1, doms)
    def _(s):
        hidden_copy(s, me, lax.rem(me + s, doms)).start()

    full[me, :, mine] = hidden[me]
    spread(me)

    @pl.loop(1, doms)
    def _(s):
        q = lax.rem(me - s + doms, doms)
        hidden_copy(s, q, lax.rem(me + s, doms)).wait_recv()
        spread(q)

    @pl.loop(0, doms)
    def _(s):
        q = lax.rem(me - s + doms, doms)
        plane(q, 0, (everything, beside), side).wait_recv()
        plane(q, 2, (upper, beside), over).start()
        plane(q, 5, (everything, beside), mate).start()
        plane(q, 1, (everything, across), over).wait_recv()
        plane(q, 3, (lower, across), side).start()
        plane(q, 6, (everything, across), mate).start()

    if small:
        count_seeds(early, total_seeds, 0)

    @pl.loop(0, doms)
    def _(s):
        q = lax.rem(me - s + doms, doms)
        plane(q, 2, (upper, corner), over).wait_recv()
        plane(q, 3, (lower, corner), side).wait_recv()
        plane(q, 7, (everything, corner), mate).start()

    local_two.wait()
    two_copy.wait_recv()

    @pl.loop(0, doms)
    def _(s):
        q = lax.rem(me - s + doms, doms)
        for k in range(4):
            plane(q, 4 + k, (everything, theirs[k]), mate).wait_recv()

    @pl.loop(0, doms // group)
    def _(part):
        block = full[pl.ds(part * group, group)].reshape(step_rows, full.shape[2])
        start = pl.multiple_of(part * step_rows, step_rows)
        rows[pl.ds(start, step_rows), :] = product(block, w_second[0]).astype(BF16)
        rows[pl.ds(known + start, step_rows), :] = product(block, w_second[1]).astype(BF16)

    @pl.loop(0, total_seeds, step=256)
    def _(start):
        start = pl.multiple_of(start, 256)
        if small:
            counted = second_c[pl.ds(start, 256), :]
        else:
            count_seeds(start, start + 256, start)
            counted = second_c[...]
        number = seeds[pl.ds(start, 256), fan_two + 1 : fan_two + 2]
        out[pl.ds(start, 256), :] = (product(counted, rows[...]) / number).astype(BF16)

    one_copy.wait_send()
    two_copy.wait_send()

    @pl.loop(1, doms)
    def _(s):
        p = lax.rem(me + s, doms)
        fetch_copy(s, me, p).wait_send()
        hidden_copy(s, me, p).wait_send()

    @pl.loop(0, doms)
    def _(q):
        pass_copy(q, core).wait_send()
        plane(q, 0, (everything, mine), side).wait_send()
        plane(q, 1, (everything, mine), over).wait_send()
        plane(q, 2, (upper, beside), over).wait_send()
        plane(q, 3, (lower, across), side).wait_send()
        plane(q, 4, (everything, mine), mate).wait_send()
        plane(q, 5, (everything, beside), mate).wait_send()
        plane(q, 6, (everything, across), mate).wait_send()
        plane(q, 7, (everything, corner), mate).wait_send()


def shards(
    doms,
    store_feat,
    want_in,
    nbr_in,
    self_in,
    count_in,
    weight_one,
    want_hid,
    nbr_hid,
    self_hid,
    count_hid,
    weight_two,
):
    stored, features = store_feat.shape
    r0, r1 = want_in.shape[2], want_hid.shape[2]
    t1, fan_one = nbr_in.shape
    t2, fan_two = nbr_hid.shape
    width = weight_one.shape[1] // 2
    columns = weight_two.shape[1]
    group = math.gcd(doms, 4)
    known = doms * r1
    counted = t2 if doms == group else 256

    def padded(fan):
        return fan + 2 + -(fan + 2) % 8

    vmem = pl.BlockSpec(memory_space=pltpu.VMEM)
    smem = pl.BlockSpec(memory_space=pltpu.SMEM)
    dma = pltpu.SemaphoreType.DMA
    return pl.pallas_call(
        functools.partial(kernel, (doms, fan_one, fan_two)),
        out_shape=jax.ShapeDtypeStruct((t2, columns), BF16),
        in_specs=[smem, smem] + [vmem] * 9,
        out_specs=vmem,
        scratch_shapes=[
            pltpu.VMEM((stored, features), F32),
            pltpu.VMEM((t1, padded(fan_one)), F32),
            pltpu.VMEM((doms * r1, padded(fan_one)), F32),
            pltpu.VMEM((doms, r0 // 2, features), BF16),
            pltpu.VMEM((doms, 2, r0 // 2, features), BF16),
            pltpu.VMEM((2, features, width), BF16),
            pltpu.VMEM((2,) + weight_two.shape, BF16),
            pltpu.VMEM((doms, r1, width), BF16),
            pltpu.VMEM((group * r1, 2 * doms * r0), BF16),
            pltpu.VMEM((doms, r1, weight_two.shape[0]), BF16),
            pltpu.VMEM((2 * known, columns), BF16),
            pltpu.VMEM((t2, padded(fan_two)), F32),
            pltpu.VMEM((counted, 2 * known), BF16),
            dma((2,)), dma((2,)), dma((2,)),
            dma((doms,)), dma((doms,)), dma((doms,)), dma((doms,)), dma((doms,)), dma((doms,)),
            dma((doms, 8)), dma((doms, 8)),
        ],
        compiler_params=pltpu.CompilerParams(
            collective_id=0, has_side_effects=True, vmem_limit_bytes=56 << 20
        ),
    )(
        want_in[0], want_hid[0], store_feat, nbr_in.T, self_in[None], count_in[None], weight_one,
        nbr_hid.T, self_hid[None], count_hid[None], weight_two,
    )


def solution(mesh):
    return jax.shard_map(
        functools.partial(shards, mesh.shape["dom"]),
        mesh=mesh,
        in_specs=(
            P("dom", None),
            P("dom", None, None),
            P("dom", None),
            P("dom"),
            P("dom"),
            P("wt", "hid"),
            P("dom", None, None),
            P("dom", None),
            P("dom"),
            P("dom"),
            P("wt", "hid"),
        ),
        out_specs=P("dom", "hid"),
        check_vma=False,
    )
```

profile of v0, /device:TPU:1, one launch (start us, length us, event | category | flops | bytes accessed | tf_op | source)
XLA Modules:
  0.0 41.5 jit_solution(5272836381922016588)
XLA Ops:
  0.0 39.2 %shard_map.109 = bf16[2048,256]{1,0:T(8,128)(2,1)} custom-call(s32[4,128]{1,0:T(4,128)} %bitcast.14, s32[4,128]{1,0:T(4,128)} %bitcast.15, bf16[4096,256]{1,0:T(8,128)(2,1)} %store.1, s32[10,8192]{1,0:T(8,128)} %bitcast.8, s32[1,8192]{1,0:T(1,128)} %bitcast.10, s32[1,8192]{1,0:T(1,128)} %bitcast.11, bf16[256,256]{1,0:T(8,128)(2,1)} %w_one.1, ...), custom_call_target="tpu_custom_call" | custom-call | tf_op jit(solution)/shard_map/pallas_call | solution.py:342
  39.2 2.3 %copy.13 = bf16[2048,256]{1,0:T(8,128)(2,1)} copy(bf16[2048,256]{1,0:T(8,128)(2,1)} %shard_map.109) | data formatting | bytes 2097152
where the time goes:
time: 41.6 us; the launch traced here: 41.5 us
  Pallas kernels  39.2 us (94%)
  local copies, waits for them, and re-layouts  2.26 us (5%)
    pallas_call x1, Pallas kernels, shards(): pl.pallas_call(functools.partial(kernel, (doms, fan_one, fan_two)), out_s...  39.2 us
    unnamed x1, local copies, waits for them, and re-layouts  2.26 us

commit v1 on v0

--- a/solution.py
+++ b/solution.py
@@ -18,14 +18,20 @@
     return jnp.dot(a, b, preferred_element_type=F32)
 
 
+def turned_product(a, b):
+    return lax.dot_general(a, b, (((0,), (0,)), ((), ())), preferred_element_type=F32)
+
+
 def tally(spots, first, last, block, weight=None):
     shifted = (spots - (block * BLOCK).astype(F32)).astype(BF16)
-    lanes = lax.broadcasted_iota(I32, (spots.shape[0], BLOCK), 1).astype(F32).astype(BF16)
-    one, none = jnp.ones((), BF16), jnp.zeros((), BF16)
-    total = jnp.zeros(lanes.shape, BF16)
-    for column in range(first, last):
-        hit = jnp.broadcast_to(shifted[:, column : column + 1], lanes.shape) == lanes
-        total = total + jnp.where(hit, one if weight is None else weight, none)
+    shape = (BLOCK, spots.shape[1])
+    lines = lax.broadcasted_iota(I32, shape, 0).astype(F32).astype(BF16)
+    none = jnp.zeros((), BF16)
+    one = jnp.ones((), BF16) if weight is None else jnp.broadcast_to(weight, shape)
+    total = jnp.zeros(shape, BF16)
+    for slot in range(first, last):
+        hit = jnp.broadcast_to(shifted[slot : slot + 1], shape) == lines
+        total = total + jnp.where(hit, one, none)
     return total
 
 
@@ -33,7 +39,7 @@
     shape,
     want_in, want_hid, store, nbr_in, self_in, count_in, w_one, nbr_hid, self_hid, count_hid, w_two,
     out,
-    storef, nodes, table, picked, fetched, w_first, w_second, hidden, first_c, full, rows, seeds, second_c,
+    storef, nodes, table, picked, fetched, w_first, w_second, hidden, first_c, full, rows, seeds, seed_count, second_c,
     local_sem, w_send, w_recv, f_send, f_recv, fc_send, fc_recv, h_send, h_recv, g_send, g_recv,
 ):
     doms, fan_one, fan_two = shape
@@ -111,65 +117,67 @@
         pad = -(fan + 2) % 8
         if pad:
             lines.append(jnp.zeros((pad, number.shape[1]), F32))
-        return jnp.concatenate(lines, 0).T
+        return jnp.concatenate(lines, 0)
 
     @pl.loop(0, nodes.shape[0], step=512)
     def _(start):
         span = pl.ds(pl.multiple_of(start, 512), 512)
-        nodes[span, :] = slots(nbr_in, self_in, count_in, fan_one, span)
+        nodes[span, :] = slots(nbr_in, self_in, count_in, fan_one, span).T
 
     @pl.loop(0, doms)
     def _(p):
         @pl.loop(0, fetch, step=8)
         def _(start):
             start = pl.multiple_of(start, 8)
-            got = [nodes[pl.ds(want_hid[p, start + i], 1), :] for i in range(8)]
-            table[pl.ds(pl.multiple_of(p * fetch, 8) + start, 8), :] = jnp.concatenate(got, 0)
-
-    @pl.loop(0, seeds.shape[0], step=512)
+            for i in range(8):
+                table[pl.ds(p * fetch + start + i, 1), :] = nodes[pl.ds(want_hid[p, start + i], 1), :]
+
+    @pl.loop(0, seeds.shape[1], step=512)
     def _(start):
         span = pl.ds(pl.multiple_of(start, 512), 512)
-        seeds[span, :] = slots(nbr_hid, self_hid, count_hid, fan_two, span)
-
-    def lanes_of(block):
-        return pl.ds(pl.multiple_of(block * BLOCK, BLOCK), BLOCK)
+        seeds[:, span] = slots(nbr_hid, self_hid, count_hid, fan_two, span)
+        number = jnp.broadcast_to(count_hid[:, span].astype(F32), (8, 512))
+        seed_count[span, :] = 1.0 / number.T
+
+    def lines_of(block, base=0):
+        return pl.ds(pl.multiple_of(base + block * BLOCK, BLOCK), BLOCK)
 
     looked = doms * fetched.shape[1] * half
     group = math.gcd(doms, 4)
     step_rows = group * fetch
 
     def count_nodes(start):
-        @pl.loop(0, step_rows, step=64)
+        @pl.loop(0, step_rows, step=128)
         def _(part):
-            part = pl.multiple_of(part, 64)
-            spots = table[pl.ds(start + part, 64), :]
+            part = pl.multiple_of(part, 128)
+            spots = table[pl.ds(start + part, 128), :].T
 
             @pl.loop(0, looked // BLOCK)
             def _(block):
-                first_c[pl.ds(part, 64), lanes_of(block)] = tally(spots, 0, fan_one, block)
-                there = pl.ds(pl.multiple_of(looked + block * BLOCK, BLOCK), BLOCK)
-                first_c[pl.ds(part, 64), there] = tally(spots, fan_one, fan_one + 1, block)
+                first_c[lines_of(block), pl.ds(part, 128)] = tally(spots, 0, fan_one, block)
+                first_c[lines_of(block, looked), pl.ds(part, 128)] = tally(
+                    spots, fan_one, fan_one + 1, block
+                )
 
     known = rows.shape[0] // 2
 
-    def count_seeds(first, last, base):
-        @pl.loop(first, last, step=64)
+    def count_seeds(first, last, base=0):
+        @pl.loop(first, last, step=128)
         def _(part):
-            part = pl.multiple_of(part, 64)
-            spots = seeds[pl.ds(part, 64), :]
-            number = spots[:, fan_two + 1 : fan_two + 2].astype(BF16)
+            part = pl.multiple_of(part, 128)
+            spots = seeds[:, pl.ds(part, 128)]
+            number = spots[fan_two + 1 : fan_two + 2].astype(BF16)
+            span = pl.ds(pl.multiple_of(part - base, 128), 128)
 
             @pl.loop(0, known // BLOCK)
             def _(block):
-                there = pl.ds(pl.multiple_of(known + block * BLOCK, BLOCK), BLOCK)
-                second_c[pl.ds(part - base, 64), lanes_of(block)] = tally(
-                    spots, fan_two, fan_two + 1, block, number
-                )
-                second_c[pl.ds(part - base, 64), there] = tally(spots, 0, fan_two, block)
+                second_c[lines_of(block), span] = tally(spots, fan_two, fan_two + 1, block, number)
+                second_c[lines_of(block, known), span] = tally(spots, 0, fan_two, block)
 
     small = doms == group
-    total_seeds = seeds.shape[0]
-    early = total_seeds // 2
+    total_seeds = seeds.shape[1]
+    share = total_seeds // (2 * doms * 128) * 128
+    early = share * (2 * doms - 1)
     if small:
         count_nodes(0)
 
@@ -178,9 +186,6 @@
         q = lax.rem(me - s + doms, doms)
         fetch_copy(s, q, lax.rem(me + s, doms)).wait_recv()
         pass_copy(q, core).start()
-
-    if small:
-        count_seeds(0, early, 0)
 
     @pl.loop(0, doms)
     def _(q):
@@ -196,8 +201,8 @@
             count_nodes(start)
         lookup = fetched[...].reshape(looked, features)
         number = table[pl.ds(start, step_rows), fan_one + 1 : fan_one + 2]
-        mean = (product(first_c[:, :looked], lookup) / number).astype(BF16)
-        own = product(first_c[:, looked:], lookup).astype(BF16)
+        mean = (turned_product(first_c[:looked], lookup) / number).astype(BF16)
+        own = turned_product(first_c[looked:], lookup).astype(BF16)
         made = product(own, w_first[0]) + product(mean, w_first[1])
         made = jnp.maximum(made, 0.0).astype(BF16)
         for i in range(group):
@@ -236,12 +241,16 @@
 
     @pl.loop(1, doms)
     def _(s):
+        if small:
+            count_seeds((s - 1) * share, s * share)
         q = lax.rem(me - s + doms, doms)
         hidden_copy(s, q, lax.rem(me + s, doms)).wait_recv()
         spread(q)
 
     @pl.loop(0, doms)
     def _(s):
+        if small:
+            count_seeds((doms - 1 + s) * share, (doms + s) * share)
         q = lax.rem(me - s + doms, doms)
         plane(q, 0, (everything, beside), side).wait_recv()
         plane(q, 2, (upper, beside), over).start()
@@ -251,7 +260,7 @@
         plane(q, 6, (everything, across), mate).start()
 
     if small:
-        count_seeds(early, total_seeds, 0)
+        count_seeds(early, total_seeds)
 
     @pl.loop(0, doms)
     def _(s):
@@ -276,16 +285,18 @@
         rows[pl.ds(start, step_rows), :] = product(block, w_second[0]).astype(BF16)
         rows[pl.ds(known + start, step_rows), :] = product(block, w_second[1]).astype(BF16)
 
-    @pl.loop(0, total_seeds, step=256)
+    chunk = 512 if small else second_c.shape[1]
+
+    @pl.loop(0, total_seeds, step=chunk)
     def _(start):
-        start = pl.multiple_of(start, 256)
+        start = pl.multiple_of(start, chunk)
         if small:
-            counted = second_c[pl.ds(start, 256), :]
+            counted = second_c[:, pl.ds(start, chunk)]
         else:
-            count_seeds(start, start + 256, start)
+            count_seeds(start, start + chunk, start)
             counted = second_c[...]
-        number = seeds[pl.ds(start, 256), fan_two + 1 : fan_two + 2]
-        out[pl.ds(start, 256), :] = (product(counted, rows[...]) / number).astype(BF16)
+        share_of_one = seed_count[pl.ds(start, chunk), :1]
+        out[pl.ds(start, chunk), :] = (turned_product(counted, rows[...]) * share_of_one).astype(BF16)
 
     one_copy.wait_send()
     two_copy.wait_send()
@@ -353,11 +364,12 @@
             pltpu.VMEM((2, features, width), BF16),
             pltpu.VMEM((2,) + weight_two.shape, BF16),
             pltpu.VMEM((doms, r1, width), BF16),
-            pltpu.VMEM((group * r1, 2 * doms * r0), BF16),
+            pltpu.VMEM((2 * doms * r0, group * r1), BF16),
             pltpu.VMEM((doms, r1, weight_two.shape[0]), BF16),
             pltpu.VMEM((2 * known, columns), BF16),
-            pltpu.VMEM((t2, padded(fan_two)), F32),
-            pltpu.VMEM((counted, 2 * known), BF16),
+            pltpu.VMEM((padded(fan_two), t2), F32),
+            pltpu.VMEM((t2, 8), F32),
+            pltpu.VMEM((2 * known, counted), BF16),
             dma((2,)), dma((2,)), dma((2,)),
             dma((doms,)), dma((doms,)), dma((doms,)), dma((doms,)), dma((doms,)), dma((doms,)),
             dma((doms, 8)), dma((doms, 8)),

time: 41.6 us -> 36.4 us (0.87)
  Pallas kernels: 39.2 us -> 34 us
    pallas_call x1, Pallas kernels: 39.2 us -> 34 us  [shards(): pl.pallas_call(functools.partial(kernel, (doms, fan_one, fan_two)), out_s...]
where the time goes in v1:
time: 36.4 us; the launch traced here: 36.3 us
  Pallas kernels  34 us (93%)
  local copies, waits for them, and re-layouts  2.26 us (6%)
    pallas_call x1, Pallas kernels, shards(): pl.pallas_call(functools.partial(kernel, (doms, fan_one, fan_two)), out_s...  34 us
    unnamed x1, local copies, waits for them, and re-layouts  2.26 us

profile of v1, /device:TPU:1, one launch (start us, length us, event | category | flops | bytes accessed | tf_op | source)
XLA Modules:
  0.0 36.3 jit_solution(15952931496707713783)
XLA Ops:
  0.0 34.0 %shard_map.109 = bf16[2048,256]{1,0:T(8,128)(2,1)} custom-call(s32[4,128]{1,0:T(4,128)} %bitcast.14, s32[4,128]{1,0:T(4,128)} %bitcast.15, bf16[4096,256]{1,0:T(8,128)(2,1)} %store.1, s32[10,8192]{1,0:T(8,128)} %bitcast.8, s32[1,8192]{1,0:T(1,128)} %bitcast.10, s32[1,8192]{1,0:T(1,128)} %bitcast.11, bf16[256,256]{1,0:T(8,128)(2,1)} %w_one.1, ...), custom_call_target="tpu_custom_call" | custom-call | tf_op jit(solution)/shard_map/pallas_call | solution.py:353
  34.0 2.3 %copy.13 = bf16[2048,256]{1,0:T(8,128)(2,1)} copy(bf16[2048,256]{1,0:T(8,128)(2,1)} %shard_map.109) | data formatting | bytes 2097152

commit v2 on v1

--- a/solution.py
+++ b/solution.py
@@ -261,6 +261,8 @@
 
     if small:
         count_seeds(early, total_seeds)
+        keep_counts = pltpu.make_async_copy(second_c, out, local_sem.at[2])
+        keep_counts.start()
 
     @pl.loop(0, doms)
     def _(s):
@@ -285,18 +287,15 @@
         rows[pl.ds(start, step_rows), :] = product(block, w_second[0]).astype(BF16)
         rows[pl.ds(known + start, step_rows), :] = product(block, w_second[1]).astype(BF16)
 
-    chunk = 512 if small else second_c.shape[1]
-
-    @pl.loop(0, total_seeds, step=chunk)
-    def _(start):
-        start = pl.multiple_of(start, chunk)
-        if small:
-            counted = second_c[:, pl.ds(start, chunk)]
-        else:
+    if not small:
+        chunk = second_c.shape[1]
+
+        @pl.loop(0, total_seeds, step=chunk)
+        def _(start):
+            start = pl.multiple_of(start, chunk)
             count_seeds(start, start + chunk, start)
-            counted = second_c[...]
-        share_of_one = seed_count[pl.ds(start, chunk), :1]
-        out[pl.ds(start, chunk), :] = (turned_product(counted, rows[...]) * share_of_one).astype(BF16)
+            made = turned_product(second_c[...], rows[...]) * seed_count[pl.ds(start, chunk), :1]
+            out[pl.ds(start, chunk), :] = made.astype(BF16)
 
     one_copy.wait_send()
     two_copy.wait_send()
@@ -318,6 +317,18 @@
         plane(q, 5, (everything, beside), mate).wait_send()
         plane(q, 6, (everything, across), mate).wait_send()
         plane(q, 7, (everything, corner), mate).wait_send()
+
+    if small:
+        keep_counts.wait()
+
+
+def split_kernel(shape, *refs):
+    inputs, (rows, seed_count, counts), rest = refs[:11], refs[11:14], refs[14:]
+    kernel(shape, *inputs, counts, *rest[:10], rows, rest[10], seed_count, *rest[11:])
+
+
+def seed_kernel(counts, rows, seed_count, out):
+    out[...] = (turned_product(counts[...], rows[...]) * seed_count[:, :1]).astype(BF16)
 
 
 def shards(
@@ -350,30 +361,42 @@
     vmem = pl.BlockSpec(memory_space=pltpu.VMEM)
     smem = pl.BlockSpec(memory_space=pltpu.SMEM)
     dma = pltpu.SemaphoreType.DMA
-    return pl.pallas_call(
-        functools.partial(kernel, (doms, fan_one, fan_two)),
-        out_shape=jax.ShapeDtypeStruct((t2, columns), BF16),
+    small = doms == group
+    scratch = [
+        pltpu.VMEM((stored, features), F32),
+        pltpu.VMEM((t1, padded(fan_one)), F32),
+        pltpu.VMEM((doms * r1, padded(fan_one)), F32),
+        pltpu.VMEM((doms, r0 // 2, features), BF16),
+        pltpu.VMEM((doms, 2, r0 // 2, features), BF16),
+        pltpu.VMEM((2, features, width), BF16),
+        pltpu.VMEM((2,) + weight_two.shape, BF16),
+        pltpu.VMEM((doms, r1, width), BF16),
+        pltpu.VMEM((2 * doms * r0, group * r1), BF16),
+        pltpu.VMEM((doms, r1, weight_two.shape[0]), BF16),
+        pltpu.VMEM((2 * known, columns), BF16),
+        pltpu.VMEM((padded(fan_two), t2), F32),
+        pltpu.VMEM((t2, 8), F32),
+        pltpu.VMEM((2 * known, counted), BF16),
+        dma((3,)), dma((2,)), dma((2,)),
+        dma((doms,)), dma((doms,)), dma((doms,)), dma((doms,)), dma((doms,)), dma((doms,)),
+        dma((doms, 8)), dma((doms, 8)),
+    ]
+    result = jax.ShapeDtypeStruct((t2, columns), BF16)
+    results, places = result, vmem
+    if small:
+        seed_count, rows = scratch.pop(12), scratch.pop(10)
+        results = (
+            jax.ShapeDtypeStruct(rows.shape, BF16),
+            jax.ShapeDtypeStruct(seed_count.shape, F32),
+            jax.ShapeDtypeStruct((2 * known, t2), BF16),
+        )
+        places = (vmem, vmem, pl.BlockSpec(memory_space=pl.ANY))
+    made = pl.pallas_call(
+        functools.partial(split_kernel if small else kernel, (doms, fan_one, fan_two)),
+        out_shape=results,
         in_specs=[smem, smem] + [vmem] * 9,
-        out_specs=vmem,
-        scratch_shapes=[
-            pltpu.VMEM((stored, features), F32),
-            pltpu.VMEM((t1, padded(fan_one)), F32),
-            pltpu.VMEM((doms * r1, padded(fan_one)), F32),
-            pltpu.VMEM((doms, r0 // 2, features), BF16),
-            pltpu.VMEM((doms, 2, r0 // 2, features), BF16),
-            pltpu.VMEM((2, features, width), BF16),
-            pltpu.VMEM((2,) + weight_two.shape, BF16),
-            pltpu.VMEM((doms, r1, width), BF16),
-            pltpu.VMEM((2 * doms * r0, group * r1), BF16),
-            pltpu.VMEM((doms, r1, weight_two.shape[0]), BF16),
-            pltpu.VMEM((2 * known, columns), BF16),
-            pltpu.VMEM((padded(fan_two), t2), F32),
-            pltpu.VMEM((t2, 8), F32),
-            pltpu.VMEM((2 * known, counted), BF16),
-            dma((2,)), dma((2,)), dma((2,)),
-            dma((doms,)), dma((doms,)), dma((doms,)), dma((doms,)), dma((doms,)), dma((doms,)),
-            dma((doms, 8)), dma((doms, 8)),
-        ],
+        out_specs=places,
+        scratch_shapes=scratch,
         compiler_params=pltpu.CompilerParams(
             collective_id=0, has_side_effects=True, vmem_limit_bytes=56 << 20
         ),
@@ -381,6 +404,22 @@
         want_in[0], want_hid[0], store_feat, nbr_in.T, self_in[None], count_in[None], weight_one,
         nbr_hid.T, self_hid[None], count_hid[None], weight_two,
     )
+    if not small:
+        return made
+    rows, seed_count, counts = made
+    chunk = math.gcd(t2, 512)
+    return pl.pallas_call(
+        seed_kernel,
+        out_shape=result,
+        grid=(t2 // chunk,),
+        in_specs=[
+            pl.BlockSpec((2 * known, chunk), lambda i: (0, i)),
+            pl.BlockSpec((2 * known, columns), lambda i: (0, 0)),
+            pl.BlockSpec((chunk, 8), lambda i: (i, 0)),
+        ],
+        out_specs=pl.BlockSpec((chunk, columns), lambda i: (i, 0)),
+        compiler_params=pltpu.CompilerParams(vmem_limit_bytes=24 << 20),
+    )(counts, rows, seed_count)
 
 
 def solution(mesh):

time: 36.4 us -> 40.1 us (1.10)
  local copies, waits for them, and re-layouts: 2.26 us -> 4.45 us
  Pallas kernels: 34 us -> 35.3 us
    unnamed x1 -> x6, local copies, waits for them, and re-layouts: 2.26 us -> 4.45 us
    pallas_call x1 -> x2, Pallas kernels: 34 us -> 35.3 us  [the longest x1 32.2 us: shards(): pl.pallas_call(functools.partial(split_kernel if small else kernel, (doms...]
where the time goes in v2:
time: 40.1 us; the launch traced here: 39.8 us
  Pallas kernels  35.3 us (88%)
  local copies, waits for them, and re-layouts  4.45 us (11%)
    pallas_call x1, Pallas kernels, shards(): pl.pallas_call(functools.partial(split_kernel if small else kernel, (doms...  32.2 us
    unnamed x6, local copies, waits for them, and re-layouts  4.45 us
    pallas_call x1, Pallas kernels, shards(): pl.pallas_call(seed_kernel, out_shape=result, grid=(t2 // chunk,), in_spe...  3.12 us

profile of v2, /device:TPU:1, one launch (start us, length us, event | category | flops | bytes accessed | tf_op | source)
XLA Modules:
  0.0 39.8 jit_solution(17204811911801991853)
XLA Ops:
  0.0 32.2 %shard_map.109 = (bf16[1024,256]{1,0:T(8,128)(2,1)}, f32[2048,8]{1,0:T(8,128)}, bf16[1024,2048]{1,0:T(8,128)(2,1)}) custom-call(s32[4,128]{1,0:T(4,128)} %bitcast.14, s32[4,128]{1,0:T(4,128)} %bitcast.15, bf16[4096,256]{1,0:T(8,128)(2,1)} %refs_2_.1, s32[10,8192]{1,0:T(8,128)} %bitcast.8, s32[1,8192]{1,0:T(1,128)} %bitcast.10, s32[1,8192]{1,0:T(1,128)} %bitcast.11, ...), custom_call_target="tpu_custom_call" | custom-call | tf_op jit(solution)/shard_map/pallas_call | solution.py:394
  32.2 0.0 copy-start
  32.2 2.2 %copy-done = bf16[1024,2048]{1,0:T(8,128)(2,1)S(1)} copy-done((bf16[1024,2048]{1,0:T(8,128)(2,1)S(1)}, bf16[1024,2048]{1,0:T(8,128)(2,1)}, u32[]{:S(2)}) %copy-start) | copy-done | bytes 4194328
  34.4 0.0 copy-start.1
  34.4 1.2 %copy-done.1 = f32[2048,8]{1,0:T(8,128)S(1)} copy-done((f32[2048,8]{1,0:T(8,128)S(1)}, f32[2048,8]{1,0:T(8,128)}, u32[]{:S(2)}) %copy-start.1) | copy-done | bytes 65560
  35.6 0.0 copy-start.2
  35.6 1.0 %copy-done.2 = bf16[1024,256]{1,0:T(8,128)(2,1)S(1)} copy-done((bf16[1024,256]{1,0:T(8,128)(2,1)S(1)}, bf16[1024,256]{1,0:T(8,128)(2,1)}, u32[]{:S(2)}) %copy-start.2) | copy-done | bytes 524312
  36.7 3.1 %shard_map.110 = bf16[2048,256]{1,0:T(8,128)(2,1)} custom-call(bf16[1024,2048]{1,0:T(8,128)(2,1)S(1)} %copy-done, bf16[1024,256]{1,0:T(8,128)(2,1)S(1)} %copy-done.2, f32[2048,8]{1,0:T(8,128)S(1)} %copy-done.1), custom_call_target="tpu_custom_call" | custom-call | tf_op jit(solution)/shard_map/pallas_call | solution.py:411
Async XLA Ops:
  32.2 2.2 %copy-start = (bf16[1024,2048]{1,0:T(8,128)(2,1)S(1)}, bf16[1024,2048]{1,0:T(8,128)(2,1)}, u32[]{:S(2)}) copy-start(bf16[1024,2048]{1,0:T(8,128)(2,1)} %get-tuple-element.8.counts) | copy-start | bytes 12582916
  34.4 1.2 %copy-start.1 = (f32[2048,8]{1,0:T(8,128)S(1)}, f32[2048,8]{1,0:T(8,128)}, u32[]{:S(2)}) copy-start(f32[2048,8]{1,0:T(8,128)} %get-tuple-element.10.seed_count) | copy-start | bytes 196612
  35.6 1.0 %copy-start.2 = (bf16[1024,256]{1,0:T(8,128)(2,1)S(1)}, bf16[1024,256]{1,0:T(8,128)(2,1)}, u32[]{:S(2)}) copy-start(bf16[1024,256]{1,0:T(8,128)(2,1)} %get-tuple-element.9.rows) | copy-start | bytes 1572868

commit v3 on v1

--- a/solution.py
+++ b/solution.py
@@ -75,28 +75,7 @@
         start = pl.multiple_of(start, 256)
         storef[pl.ds(start, 256), :] = store[pl.ds(start, 256), :].astype(F32)
 
-    @pl.loop(0, doms)
-    def _(p):
-        @pl.loop(0, half, step=16)
-        def _(start):
-            start = pl.multiple_of(start, 16)
-            got = [storef[pl.ds(want_in[p, core * half + start + i], 1), :] for i in range(16)]
-            picked[p, pl.ds(start, 16), :] = jnp.concatenate(got, 0).astype(BF16)
-
     pl.semaphore_wait(barrier, doms + 2)
-
-    def fetch_copy(s, q, p):
-        return remote(picked.at[p], fetched.at[q, core], f_send.at[s], f_recv.at[s], {"dom": p})
-
-    def pass_copy(q, c):
-        return remote(fetched.at[q, c], fetched.at[q, c], fc_send.at[q], fc_recv.at[q], mate)
-
-    @pl.loop(1, doms)
-    def _(s):
-        fetch_copy(s, me, lax.rem(me + s, doms)).start()
-
-    fetched[me, core] = picked[me]
-    pass_copy(me, core).start()
 
     their_columns = pl.ds(pl.multiple_of((1 - w) * width, width), width)
     my_columns = pl.ds(pl.multiple_of(w * width, width), width)
@@ -108,6 +87,27 @@
     local_two = pltpu.make_async_copy(w_two, w_second.at[w], local_sem.at[1])
     local_one.start()
     local_two.start()
+
+    @pl.loop(0, doms)
+    def _(p):
+        @pl.loop(0, half, step=16)
+        def _(start):
+            start = pl.multiple_of(start, 16)
+            got = [storef[pl.ds(want_in[p, core * half + start + i], 1), :] for i in range(16)]
+            picked[p, pl.ds(start, 16), :] = jnp.concatenate(got, 0).astype(BF16)
+
+    def fetch_copy(s, q, p):
+        return remote(picked.at[p], fetched.at[q, core], f_send.at[s], f_recv.at[s], {"dom": p})
+
+    def pass_copy(q, c):
+        return remote(fetched.at[q, c], fetched.at[q, c], fc_send.at[q], fc_recv.at[q], mate)
+
+    @pl.loop(1, doms)
+    def _(s):
+        fetch_copy(s, me, lax.rem(me + s, doms)).start()
+
+    fetched[me, core] = picked[me]
+    pass_copy(me, core).start()
 
     def slots(neighbours, own, counts, fan, span):
         number = counts[:, span]
@@ -225,7 +225,7 @@
     def plane(q, k, view, where):
         return remote(full.at[q, view[0], view[1]], full.at[q, view[0], view[1]], g_send.at[q, k], g_recv.at[q, k], where)
 
-    everything, upper, lower = pl.ds(0, fetch), pl.ds(0, fetch // 2), pl.ds(fetch // 2, fetch // 2)
+    everything = pl.ds(0, fetch)
 
     def spread(q):
         plane(q, 0, (everything, mine), side).start()
@@ -253,10 +253,9 @@
             count_seeds((doms - 1 + s) * share, (doms + s) * share)
         q = lax.rem(me - s + doms, doms)
         plane(q, 0, (everything, beside), side).wait_recv()
-        plane(q, 2, (upper, beside), over).start()
         plane(q, 5, (everything, beside), mate).start()
         plane(q, 1, (everything, across), over).wait_recv()
-        plane(q, 3, (lower, across), side).start()
+        plane(q, 3, (everything, across), side).start()
         plane(q, 6, (everything, across), mate).start()
 
     if small:
@@ -265,12 +264,10 @@
     @pl.loop(0, doms)
     def _(s):
         q = lax.rem(me - s + doms, doms)
-        plane(q, 2, (upper, corner), over).wait_recv()
-        plane(q, 3, (lower, corner), side).wait_recv()
+        plane(q, 3, (everything, corner), side).wait_recv()
         plane(q, 7, (everything, corner), mate).start()
 
     local_two.wait()
-    two_copy.wait_recv()
 
     @pl.loop(0, doms)
     def _(s):
@@ -282,8 +279,17 @@
     def _(part):
         block = full[pl.ds(part * group, group)].reshape(step_rows, full.shape[2])
         start = pl.multiple_of(part * step_rows, step_rows)
-        rows[pl.ds(start, step_rows), :] = product(block, w_second[0]).astype(BF16)
-        rows[pl.ds(known + start, step_rows), :] = product(block, w_second[1]).astype(BF16)
+        there = pl.ds(pl.multiple_of(w * known + start, step_rows), step_rows)
+        rows[there, :] = product(block, w_second[w]).astype(BF16)
+
+    two_copy.wait_recv()
+
+    @pl.loop(0, doms // group)
+    def _(part):
+        block = full[pl.ds(part * group, group)].reshape(step_rows, full.shape[2])
+        start = pl.multiple_of(part * step_rows, step_rows)
+        there = pl.ds(pl.multiple_of((1 - w) * known + start, step_rows), step_rows)
+        rows[there, :] = product(block, w_second[1 - w]).astype(BF16)
 
     chunk = 512 if small else second_c.shape[1]
 
@@ -312,8 +318,7 @@
         pass_copy(q, core).wait_send()
         plane(q, 0, (everything, mine), side).wait_send()
         plane(q, 1, (everything, mine), over).wait_send()
-        plane(q, 2, (upper, beside), over).wait_send()
-        plane(q, 3, (lower, across), side).wait_send()
+        plane(q, 3, (everything, across), side).wait_send()
         plane(q, 4, (everything, mine), mate).wait_send()
         plane(q, 5, (everything, beside), mate).wait_send()
         plane(q, 6, (everything, across), mate).wait_send()

time: 36.4 us -> 37.1 us (1.019)
  Pallas kernels: 34 us -> 34.6 us
    pallas_call x1, Pallas kernels: 34 us -> 34.6 us  [shards(): pl.pallas_call(functools.partial(kernel, (doms, fan_one, fan_two)), out_s...]
where the time goes in v3:
time: 37.1 us; the launch traced here: 36.9 us
  Pallas kernels  34.6 us (93%)
  local copies, waits for them, and re-layouts  2.26 us (6%)
    pallas_call x1, Pallas kernels, shards(): pl.pallas_call(functools.partial(kernel, (doms, fan_one, fan_two)), out_s...  34.6 us
    unnamed x1, local copies, waits for them, and re-layouts  2.26 us

profile of v3, /device:TPU:1, one launch (start us, length us, event | category | flops | bytes accessed | tf_op | source)
XLA Modules:
  0.0 36.9 jit_solution(6763450278764068383)
XLA Ops:
  0.0 34.6 %shard_map.109 = bf16[2048,256]{1,0:T(8,128)(2,1)} custom-call(s32[4,128]{1,0:T(4,128)} %bitcast.14, s32[4,128]{1,0:T(4,128)} %bitcast.15, bf16[4096,256]{1,0:T(8,128)(2,1)} %store.1, s32[10,8192]{1,0:T(8,128)} %bitcast.8, s32[1,8192]{1,0:T(1,128)} %bitcast.10, s32[1,8192]{1,0:T(1,128)} %bitcast.11, bf16[256,256]{1,0:T(8,128)(2,1)} %w_one.1, ...), custom_call_target="tpu_custom_call" | custom-call | tf_op jit(solution)/shard_map/pallas_call | solution.py:358
  34.6 2.3 %copy.13 = bf16[2048,256]{1,0:T(8,128)(2,1)} copy(bf16[2048,256]{1,0:T(8,128)(2,1)} %shard_map.109) | data formatting | bytes 2097152
